TPU v7x, 512 devices: a whole 4x4x16 slice. The times are simulated.
512 devices in a mesh: leaf: 128 (over z, y, core), list: 4 (over x).
Axes of the slice: x: 4, y: 4, z: 16, core: 2. Of those that a mesh axis runs over, the one named last changes fastest.
Arguments:
- charge: float32 [256, 32768], P('list', 'leaf'), may hold values from -3 to 3
- position: float32 [3, 256, 32768], P(None, 'list', 'leaf'), may hold values from -1 to 1
- charge_count: int32 [32768], P('leaf'), may hold values from 0 to 256, as said below
- octant: int32 [36864], P('leaf'), may hold values from 0 to 7, as said below
- shift_ops: bfloat16 [8, 28672], replicated, may hold values from -0.15625 to 0.15625
- m2l_ops: bfloat16 [160, 28672], P('list'), may hold values from -0.0390625 to 0.0390625
- let_send: int32 [128, 8, 128], P('leaf'), may hold values from 0 to 255
- list_src: int32 [128, 160, 384], P('leaf', 'list'), may hold values from 0 to 1279, as said below
- list_dst: int32 [128, 160, 384], P('leaf', 'list'), may hold values from 0 to 255
- batch_count: int32 [128, 160], P('leaf', 'list'), may hold values from 192 to 384, as said below
Outputs:
- local_field: bfloat16 [169, 32768], P(None, ('leaf', 'list'))
- tree_multipoles: bfloat16 [169, 4608], P(None, 'leaf')
Inputs may be any that keep to these rules, and one draw needn't show every extreme that they name: `charge_count`: the first leaf of each index of leaf has 256 occupied slots. `octant`: each aligned group of 8 entries is a permutation of 0 to 7. `list_src`: a column 256 + k * 128 + c is used only where d + off(k) is an index of leaf. `batch_count`: every index of leaf has one full batch.
All inputs are finite; a program needn't handle non-finite values.
Results may differ from a plain program's by a relative error of at most 0.0051.
Values may be sent and summed in bfloat16 or wider, within the bound.
A program may use at most 64 MiB of HBM per device.

v0:
```python
import functools

import jax
import jax.numpy as jnp
from jax import lax
from jax.experimental import pallas as pl
from jax.experimental.pallas import tpu as pltpu
from jax.sharding import PartitionSpec as P

ORDER = 12
NCOEF = (ORDER + 1) ** 2
ROWS = 176
CHUNK = 48
LEAF = 256
CAP = 128
NEAR = 8
BATCH = 384
OCT = 8
WIDE = 256
HALF = ROWS // 2

MESH = pl.DeviceIdType.MESH
F32 = jnp.float32
BF16 = jnp.bfloat16
NT = (((1,), (1,)), ((), ()))


def iota(shape, dim):
    return lax.broadcasted_iota(jnp.int32, shape, dim)


def onehot(mask):
    return jnp.where(mask, 1.0, 0.0).astype(BF16)


def dot(a, b):
    return jnp.dot(a, b, preferred_element_type=F32)


def dot_nt(a, b):
    return lax.dot_general(a, b, NT, preferred_element_type=F32)


def kernel(
    n_leaf,
    n_list,
    charge,
    position,
    count,
    octant,
    shift_ops,
    m2l_ops,
    let_send,
    list_src,
    list_dst,
    batch_count,
    local_out,
    tree_out,
    tz,
    tx,
    ty,
    acc,
    part,
    rs_buf,
    multi,
    outgoing,
    table,
    flat0,
    flat1,
    m_cat,
    s_cat,
    pick,
    z_cat,
    total,
    fin,
    fin_buf,
    rs_send,
    rs_recv,
    ag_send,
    ag_recv,
    halo_send,
    halo_recv,
    fin_send,
    fin_recv,
):
    n_ops = m2l_ops.shape[0]
    all_ops = n_ops + OCT
    slots = charge.shape[0]
    me_leaf = lax.axis_index("leaf")
    me = lax.axis_index("list")
    offsets = [k - NEAR // 2 if k < NEAR // 2 else k - NEAR // 2 + 1 for k in range(NEAR)]
    near_ids = [lax.rem(me_leaf + off + n_leaf, n_leaf) for off in offsets]
    peers = [lax.rem(me + r, n_list) for r in range(1, n_list)]

    barrier = pltpu.get_barrier_semaphore()
    for near in near_ids:
        pl.semaphore_signal(barrier, inc=1, device_id=(near, me), device_id_type=MESH)
    for peer in peers:
        pl.semaphore_signal(barrier, inc=1, device_id=(me_leaf, peer), device_id_type=MESH)

    slot_ids = me * slots + iota((slots, LEAF), 0)
    q = jnp.where(slot_ids < count[...], charge[...], 0.0)
    for axis, dst in ((0, tx), (1, ty), (2, tz)):
        v = position[axis]
        scale = q if axis == 2 else jnp.ones_like(v)
        prev, cur = scale, v * scale
        dst[0] = prev
        dst[1] = cur
        for n in range(2, ORDER + 1):
            prev, cur = cur, 2.0 * v * cur - prev
            dst[n] = cur
    for lane in range(LEAF // 128):
        cols = slice(lane * 128, lane * 128 + 128)
        acc[lane, NCOEF * 8 :, :] = jnp.zeros((acc.shape[1] - NCOEF * 8, 128), F32)
        for n in range(ORDER + 1):
            zn = tz[n, :, cols]
            for m in range(-n, n + 1):
                c = n * n + n + m
                if m > 0:
                    term = zn * tx[m, :, cols]
                elif m < 0:
                    term = zn * ty[-m, :, cols]
                else:
                    term = zn
                acc[lane, c * 8 : c * 8 + 8, :] = jnp.sum(term.reshape(slots // 8, 8, 128), axis=0)
        for chunk in range(n_list):
            s = acc[lane, pl.ds(chunk * CHUNK * 8, CHUNK, stride=8), :]
            for i in range(1, 8):
                s = s + acc[lane, pl.ds(chunk * CHUNK * 8 + i, CHUNK, stride=8), :]
            part[chunk, :, cols] = s

    pl.semaphore_wait(barrier, NEAR + n_list - 1)

    rs = []
    for r in range(1, n_list):
        copy = pltpu.make_async_remote_copy(
            src_ref=part.at[peers[r - 1]],
            dst_ref=rs_buf.at[r - 1],
            send_sem=rs_send.at[r - 1],
            recv_sem=rs_recv.at[r - 1],
            device_id=(me_leaf, peers[r - 1]),
            device_id_type=MESH,
        )
        copy.start()
        rs.append(copy)

    tail = pl.ds(NCOEF * all_ops, (ROWS - NCOEF) * all_ops)
    flat0[tail, :] = jnp.zeros(((ROWS - NCOEF) * all_ops, 128), F32)
    flat1[tail, :] = jnp.zeros(((ROWS - NCOEF) * all_ops, 128), F32)

    def align_row(k, _):
        start = k * NCOEF
        first = start // 128
        turn = start - first * 128
        back = lax.rem(128 - turn, 128)
        for ref, at in ((m2l_ops, 0), (shift_ops, n_ops)):
            count_ops = ref.shape[0]
            lanes = iota((count_ops, 128), 1)
            pieces = [
                pltpu.roll(
                    ref[:, pl.ds(pl.multiple_of((first + i) * 128, 128), 128)].astype(F32), back, 1
                )
                for i in range(3)
            ]
            keep = lanes < 128 - turn
            rows = pl.ds(pl.multiple_of(k * all_ops + at, 8), count_ops)
            flat0[rows, :] = jnp.where(keep, pieces[0], pieces[1])
            flat1[rows, :] = jnp.where(
                lanes < NCOEF - 128, jnp.where(keep, pieces[1], pieces[2]), 0.0
            )
        return 0

    lax.fori_loop(0, NCOEF, align_row, 0)

    for copy in rs:
        copy.wait()
    mine = part[me]
    for r in range(1, n_list):
        mine = mine + rs_buf[r - 1]
    multi[me] = mine.astype(BF16)
    ag = []
    for r in range(1, n_list):
        copy = pltpu.make_async_remote_copy(
            src_ref=multi.at[me],
            dst_ref=multi.at[me],
            send_sem=ag_send.at[r - 1],
            recv_sem=ag_recv.at[r - 1],
            device_id=(me_leaf, peers[r - 1]),
            device_id_type=MESH,
        )
        copy.start()
        ag.append(copy)

    def take_op(g, _):
        cols = pl.multiple_of(g * WIDE, WIDE)
        m_cat[:, pl.ds(cols, 128)] = flat0[pl.ds(g, ROWS, stride=all_ops), :].astype(BF16)
        m_cat[:, pl.ds(cols + 128, 128)] = flat1[pl.ds(g, ROWS, stride=all_ops), :].astype(BF16)
        return 0

    lax.fori_loop(0, n_ops, take_op, 0)
    for o in range(OCT):
        rows = pl.ds(n_ops + o, ROWS, stride=all_ops)
        s_cat[:, o * WIDE : o * WIDE + 128] = flat0[rows, :].astype(BF16)
        s_cat[:, o * WIDE + 128 : o * WIDE + 256] = flat1[rows, :].astype(BF16)

    for copy in ag:
        copy.wait()
    leaves = multi[...].reshape(n_list * CHUNK, LEAF)[:ROWS]
    table[:, :LEAF] = leaves

    halo = []
    for k in (0, 7, 1, 6, 2, 5, 3, 4):
        pickers = onehot(iota((LEAF, CAP), 0) == let_send[k : k + 1, :])
        outgoing[k] = dot(leaves, pickers).astype(BF16)
        to = LEAF + (NEAR - 1 - k) * CAP
        copy = pltpu.make_async_remote_copy(
            src_ref=outgoing.at[k],
            dst_ref=table.at[:, to : to + CAP],
            send_sem=halo_send.at[k],
            recv_sem=halo_recv.at[k],
            device_id=(near_ids[k], me),
            device_id_type=MESH,
        )
        copy.start()
        halo.append(copy)

    pick[...] = jnp.zeros_like(pick)
    child = iota((128, LEAF), 1)
    cell = iota((128, LEAF), 0)
    octs = octant[0:1, 0:LEAF]
    for o in range(OCT):
        chosen = onehot(cell == jnp.where(octs == o, child // 8, -1))
        pick[o * WIDE : o * WIDE + ROWS, :] = dot_nt(leaves, chosen).astype(BF16)
    parents = dot(s_cat[...], pick[...]).astype(BF16)
    n_par = LEAF // 8
    child = iota((128, n_par), 1)
    cell = iota((128, n_par), 0)
    octs = octant[0:1, LEAF : LEAF + n_par]
    for o in range(OCT):
        chosen = onehot(cell == jnp.where(octs == o, n_par + child // 8, -1))
        pick[o * WIDE : o * WIDE + ROWS, :] = dot_nt(parents[:, :n_par], chosen).astype(BF16)
    grand = dot(s_cat[...], pick[...])
    tree = jnp.where(iota((ROWS, 128), 1) < n_par, parents.astype(F32), grand).astype(BF16)
    tree_out[...] = tree[:NCOEF, : n_par + n_par // 8]

    for copy in halo:
        copy.wait()

    def gather_op(g, _):
        src = list_src[pl.ds(g, 1), :]
        dst = list_dst[pl.ds(g, 1), :]
        src = jnp.where(iota((1, BATCH), 1) < batch_count[0, g], src, -1)
        x = jnp.zeros((ROWS, BATCH), F32)
        for h in range(table.shape[1] // 256):
            hot = onehot(iota((256, BATCH), 0) + h * 256 == src)
            x = x + dot(table[:, h * 256 : h * 256 + 256], hot)
        hot = onehot(iota((LEAF, BATCH), 0) == dst)
        z = dot_nt(x.astype(BF16), hot).astype(BF16)
        z_cat[pl.ds(pl.multiple_of(g * WIDE, WIDE), ROWS), :] = z
        z_cat[pl.ds(pl.multiple_of(g * WIDE + ROWS, 16), WIDE - ROWS), :] = jnp.zeros(
            (WIDE - ROWS, LEAF), BF16
        )
        return 0

    lax.fori_loop(0, n_ops, gather_op, 0)
    total[...] = dot(m_cat[...], z_cat[...])

    left = iota((HALF, 128), 1) < 64
    for j in range(n_list):
        cols = slice(j // 2 * 128, j // 2 * 128 + 128)
        top, low = total[:HALF, cols], total[HALF:, cols]
        if j % 2 == 0:
            fin[j] = jnp.where(left, top, pltpu.roll(low, 64, 1))
        else:
            fin[j] = jnp.where(left, pltpu.roll(top, 64, 1), low)
    last = []
    for r in range(1, n_list):
        copy = pltpu.make_async_remote_copy(
            src_ref=fin.at[peers[r - 1]],
            dst_ref=fin_buf.at[r - 1],
            send_sem=fin_send.at[r - 1],
            recv_sem=fin_recv.at[r - 1],
            device_id=(me_leaf, peers[r - 1]),
            device_id_type=MESH,
        )
        copy.start()
        last.append(copy)
    for copy in last:
        copy.wait()
    s = fin[me]
    for r in range(1, n_list):
        s = s + fin_buf[r - 1]
    local_out[:HALF, :] = s[:, :64].astype(BF16)
    local_out[HALF:, :] = pltpu.roll(s, 64, 1)[: NCOEF - HALF, :64].astype(BF16)


def per_device(
    n_leaf,
    n_list,
    charge,
    position,
    charge_count,
    octant,
    shift_ops,
    m2l_ops,
    let_send,
    list_src,
    list_dst,
    batch_count,
):
    slots = charge.shape[0]
    n_ops = m2l_ops.shape[0]
    all_ops = n_ops + OCT
    columns = LEAF + NEAR * CAP
    vmem = pl.BlockSpec(memory_space=pltpu.VMEM)
    dma = pltpu.SemaphoreType.DMA
    return pl.pallas_call(
        functools.partial(kernel, n_leaf, n_list),
        out_shape=(
            jax.ShapeDtypeStruct((NCOEF, LEAF // n_list), BF16),
            jax.ShapeDtypeStruct((NCOEF, LEAF // 8 + LEAF // 64), BF16),
        ),
        in_specs=[vmem] * 9 + [pl.BlockSpec(memory_space=pltpu.SMEM)],
        out_specs=(vmem, vmem),
        scratch_shapes=[
            pltpu.VMEM((ORDER + 1, slots, LEAF), F32),
            pltpu.VMEM((ORDER + 1, slots, LEAF), F32),
            pltpu.VMEM((ORDER + 1, slots, LEAF), F32),
            pltpu.VMEM((LEAF // 128, n_list * CHUNK * 8, 128), F32),
            pltpu.VMEM((n_list, CHUNK, LEAF), F32),
            pltpu.VMEM((n_list - 1, CHUNK, LEAF), F32),
            pltpu.VMEM((n_list, CHUNK, LEAF), BF16),
            pltpu.VMEM((NEAR, ROWS, CAP), BF16),
            pltpu.VMEM((ROWS, columns), BF16),
            pltpu.VMEM((ROWS * all_ops, 128), F32),
            pltpu.VMEM((ROWS * all_ops, 128), F32),
            pltpu.VMEM((ROWS, n_ops * WIDE), BF16),
            pltpu.VMEM((ROWS, OCT * WIDE), BF16),
            pltpu.VMEM((OCT * WIDE, 128), BF16),
            pltpu.VMEM((n_ops * WIDE, LEAF), BF16),
            pltpu.VMEM((ROWS, LEAF), F32),
            pltpu.VMEM((n_list, HALF, 128), F32),
            pltpu.VMEM((n_list - 1, HALF, 128), F32),
            dma((n_list - 1,)),
            dma((n_list - 1,)),
            dma((n_list - 1,)),
            dma((n_list - 1,)),
            dma((NEAR,)),
            dma((NEAR,)),
            dma((n_list - 1,)),
            dma((n_list - 1,)),
        ],
        compiler_params=pltpu.CompilerParams(
            collective_id=0, has_side_effects=True, vmem_limit_bytes=56 << 20
        ),
    )(
        charge,
        position,
        charge_count.reshape(1, -1),
        octant.reshape(1, -1),
        shift_ops,
        m2l_ops,
        let_send[0],
        list_src[0],
        list_dst[0],
        batch_count,
    )


def solution(mesh):
    return jax.shard_map(
        functools.partial(per_device, mesh.shape["leaf"], mesh.shape["list"]),
        mesh=mesh,
        in_specs=(
            P("list", "leaf"),
            P(None, "list", "leaf"),
            P("leaf"),
            P("leaf"),
            P(),
            P("list", None),
            P("leaf", None, None),
            P("leaf", "list", None),
            P("leaf", "list", None),
            P("leaf", "list"),
        ),
        out_specs=(P(None, ("leaf", "list")), P(None, "leaf")),
        check_vma=False,
    )
```

profile of v0, /device:TPU:1, one launch (start us, length us, event | category | flops | bytes accessed | tf_op | source)
XLA Modules:
  0.0 76.4 jit_solution(10552220953209616700)
XLA Ops:
  0.6 1.2 %reshape.11.octant = s32[1,288]{1,0:T(1,128)} reshape(s32[288]{0:T(512)} %param.13) | data formatting | bytes 2304 | tf_op jit(solution)/shard_map/reshape | solution.py:360
  1.9 71.5 %shard_map.113 = (bf16[169,64]{1,0:T(8,128)(2,1)}, bf16[169,36]{1,0:T(8,128)(2,1)}) custom-call(f32[64,256]{1,0:T(8,128)} %charge.1, f32[3,64,256]{2,1,0:T(8,128)} %position.1, s32[1,256]{1,0:T(1,128)} %bitcast.7, s32[1,288]{1,0:T(1,128)} %reshape.11.octant, bf16[8,28672]{1,0:T(8,128)(2,1)} %shift_ops.1, bf16[40,28672]{1,0:T(8,128)(2,1)} %m2l_ops.1, ...), custom_call_target="tpu_custom_call" | custom-call | tf_op jit(solution)/shard_map/pallas_call | solution.py:317
  73.4 1.5 %copy.12 = bf16[169,64]{0,1:T(8,128)(2,1)} copy(bf16[169,64]{1,0:T(8,128)(2,1)} %get-tuple-element.2) | data formatting | bytes 43264 | tf_op jit(solution)/shard_map/pallas_call | solution.py:317
  74.9 1.5 %copy.13 = bf16[169,36]{0,1:T(8,128)(2,1)} copy(bf16[169,36]{1,0:T(8,128)(2,1)} %get-tuple-element.3) | data formatting | bytes 24336 | tf_op jit(solution)/shard_map/pallas_call | solution.py:317
where the time goes:
time: 76.7 us; the launch traced here: 76.4 us
  Pallas kernels  71.5 us (93%)
  local copies, waits for them, and re-layouts  4.23 us (6%)
    pallas_call x1, Pallas kernels, per_device(): pl.pallas_call(functools.partial(kernel, n_leaf, n_list), out_shape=(jax....  71.5 us
    pallas_call x2, local copies, waits for them, and re-layouts, per_device(): pl.pallas_call(functools.partial(kernel, n_leaf, n_list), out_shape=(jax....  2.98 us

commit v1 on v0

--- a/solution.py
+++ b/solution.py
@@ -18,6 +18,9 @@
 OCT = 8
 WIDE = 256
 HALF = ROWS // 2
+BLOCK = 4
+IN_PARTS = 4
+SPREAD = 56
 
 MESH = pl.DeviceIdType.MESH
 F32 = jnp.float32
@@ -44,18 +47,24 @@
 def kernel(
     n_leaf,
     n_list,
-    charge,
-    position,
+    charge_hbm,
+    position_hbm,
     count,
     octant,
-    shift_ops,
-    m2l_ops,
+    shift_hbm,
+    m2l_hbm,
     let_send,
-    list_src,
-    list_dst,
+    src_hbm,
+    dst_hbm,
     batch_count,
     local_out,
     tree_out,
+    charge,
+    position,
+    shift_ops,
+    m2l_ops,
+    list_src,
+    list_dst,
     tz,
     tx,
     ty,
@@ -70,7 +79,8 @@
     m_cat,
     s_cat,
     pick,
-    z_cat,
+    x_buf,
+    z_buf,
     total,
     fin,
     fin_buf,
@@ -82,9 +92,10 @@
     halo_recv,
     fin_send,
     fin_recv,
+    in_sem,
 ):
     n_ops = m2l_ops.shape[0]
-    all_ops = n_ops + OCT
+    all_ops = SPREAD
     slots = charge.shape[0]
     me_leaf = lax.axis_index("leaf")
     me = lax.axis_index("list")
@@ -92,12 +103,35 @@
     near_ids = [lax.rem(me_leaf + off + n_leaf, n_leaf) for off in offsets]
     peers = [lax.rem(me + r, n_list) for r in range(1, n_list)]
 
+    charges_in = [
+        pltpu.make_async_copy(charge_hbm, charge, in_sem.at[0]),
+        pltpu.make_async_copy(position_hbm, position, in_sem.at[1]),
+    ]
+    step = m2l_ops.shape[1] // IN_PARTS
+    ops_in = [
+        pltpu.make_async_copy(
+            m2l_hbm.at[:, i * step : i * step + step],
+            m2l_ops.at[:, i * step : i * step + step],
+            in_sem.at[5 + i],
+        )
+        for i in range(IN_PARTS)
+    ]
+    lists_in = [
+        pltpu.make_async_copy(src_hbm, list_src, in_sem.at[3]),
+        pltpu.make_async_copy(dst_hbm, list_dst, in_sem.at[4]),
+    ]
+    ops_in.append(pltpu.make_async_copy(shift_hbm, shift_ops, in_sem.at[2]))
+    for copy in charges_in + ops_in + lists_in:
+        copy.start()
+
     barrier = pltpu.get_barrier_semaphore()
     for near in near_ids:
         pl.semaphore_signal(barrier, inc=1, device_id=(near, me), device_id_type=MESH)
     for peer in peers:
         pl.semaphore_signal(barrier, inc=1, device_id=(me_leaf, peer), device_id_type=MESH)
 
+    for copy in charges_in:
+        copy.wait()
     slot_ids = me * slots + iota((slots, LEAF), 0)
     q = jnp.where(slot_ids < count[...], charge[...], 0.0)
     for axis, dst in ((0, tx), (1, ty), (2, tz)):
@@ -170,7 +204,9 @@
             )
         return 0
 
-    lax.fori_loop(0, NCOEF, align_row, 0)
+    for copy in ops_in:
+        copy.wait()
+    lax.fori_loop(0, 91, align_row, 0, unroll=13)
 
     for copy in rs:
         copy.wait()
@@ -191,17 +227,7 @@
         copy.start()
         ag.append(copy)
 
-    def take_op(g, _):
-        cols = pl.multiple_of(g * WIDE, WIDE)
-        m_cat[:, pl.ds(cols, 128)] = flat0[pl.ds(g, ROWS, stride=all_ops), :].astype(BF16)
-        m_cat[:, pl.ds(cols + 128, 128)] = flat1[pl.ds(g, ROWS, stride=all_ops), :].astype(BF16)
-        return 0
-
-    lax.fori_loop(0, n_ops, take_op, 0)
-    for o in range(OCT):
-        rows = pl.ds(n_ops + o, ROWS, stride=all_ops)
-        s_cat[:, o * WIDE : o * WIDE + 128] = flat0[rows, :].astype(BF16)
-        s_cat[:, o * WIDE + 128 : o * WIDE + 256] = flat1[rows, :].astype(BF16)
+    lax.fori_loop(91, NCOEF, align_row, 0, unroll=13)
 
     for copy in ag:
         copy.wait()
@@ -224,10 +250,22 @@
         copy.start()
         halo.append(copy)
 
+    def take_op(g, _):
+        cols = pl.multiple_of(g * WIDE, WIDE)
+        m_cat[:, pl.ds(cols, 128)] = flat0[pl.ds(g, ROWS, stride=all_ops), :].astype(BF16)
+        m_cat[:, pl.ds(cols + 128, 128)] = flat1[pl.ds(g, ROWS, stride=all_ops), :].astype(BF16)
+        return 0
+
+    lax.fori_loop(0, n_ops, take_op, 0, unroll=4)
+    for o in range(OCT):
+        rows = pl.ds(n_ops + o, ROWS, stride=all_ops)
+        s_cat[:, o * WIDE : o * WIDE + 128] = flat0[rows, :].astype(BF16)
+        s_cat[:, o * WIDE + 128 : o * WIDE + 256] = flat1[rows, :].astype(BF16)
+
     pick[...] = jnp.zeros_like(pick)
     child = iota((128, LEAF), 1)
     cell = iota((128, LEAF), 0)
-    octs = octant[0:1, 0:LEAF]
+    octs = octant[pl.ds(0, LEAF)].reshape(1, LEAF)
     for o in range(OCT):
         chosen = onehot(cell == jnp.where(octs == o, child // 8, -1))
         pick[o * WIDE : o * WIDE + ROWS, :] = dot_nt(leaves, chosen).astype(BF16)
@@ -235,35 +273,61 @@
     n_par = LEAF // 8
     child = iota((128, n_par), 1)
     cell = iota((128, n_par), 0)
-    octs = octant[0:1, LEAF : LEAF + n_par]
+    octs = octant[pl.ds(LEAF, n_par)].reshape(1, n_par)
     for o in range(OCT):
         chosen = onehot(cell == jnp.where(octs == o, n_par + child // 8, -1))
         pick[o * WIDE : o * WIDE + ROWS, :] = dot_nt(parents[:, :n_par], chosen).astype(BF16)
     grand = dot(s_cat[...], pick[...])
-    tree = jnp.where(iota((ROWS, 128), 1) < n_par, parents.astype(F32), grand).astype(BF16)
-    tree_out[...] = tree[:NCOEF, : n_par + n_par // 8]
+    tree = jnp.where(iota((ROWS, 128), 1) < n_par, parents.astype(F32), grand)
+    tree_out[...] = tree.T[: n_par + n_par // 8, :NCOEF].astype(BF16)
 
     for copy in halo:
         copy.wait()
 
-    def gather_op(g, _):
-        src = list_src[pl.ds(g, 1), :]
-        dst = list_dst[pl.ds(g, 1), :]
-        src = jnp.where(iota((1, BATCH), 1) < batch_count[0, g], src, -1)
-        x = jnp.zeros((ROWS, BATCH), F32)
-        for h in range(table.shape[1] // 256):
-            hot = onehot(iota((256, BATCH), 0) + h * 256 == src)
-            x = x + dot(table[:, h * 256 : h * 256 + 256], hot)
-        hot = onehot(iota((LEAF, BATCH), 0) == dst)
-        z = dot_nt(x.astype(BF16), hot).astype(BF16)
-        z_cat[pl.ds(pl.multiple_of(g * WIDE, WIDE), ROWS), :] = z
-        z_cat[pl.ds(pl.multiple_of(g * WIDE + ROWS, 16), WIDE - ROWS), :] = jnp.zeros(
-            (WIDE - ROWS, LEAF), BF16
-        )
+    for copy in lists_in:
+        copy.wait()
+
+    def hot16(row, base, n):
+        ids = iota((n, row.shape[1]), 0).astype(jnp.int16)
+        return jnp.where(ids == (row - base).astype(jnp.int16), jnp.array(1, BF16), jnp.array(0, BF16))
+
+    def gather(i):
+        for u in range(BLOCK):
+            g = i * BLOCK + u
+            src = list_src[pl.ds(g, 1), :]
+            src = jnp.where(iota((1, BATCH), 1) < batch_count[0, g], src, -1)
+            x = jnp.zeros((ROWS, BATCH), F32)
+            for h in range(table.shape[1] // 256):
+                x = x + dot(table[:, h * 256 : h * 256 + 256], hot16(src, h * 256, 256))
+            x_buf[lax.rem(i, 2), u] = x.astype(BF16)
+
+    def scatter(i):
+        for u in range(BLOCK):
+            dst = list_dst[pl.ds(i * BLOCK + u, 1), :]
+            z = dot_nt(x_buf[lax.rem(i, 2), u], hot16(dst, 0, LEAF))
+            z_buf[lax.rem(i, 2), u * WIDE : u * WIDE + ROWS, :] = z.astype(BF16)
+
+    def apply(i):
+        cols = pl.ds(pl.multiple_of(i * (BLOCK * WIDE), BLOCK * WIDE), BLOCK * WIDE)
+        total[...] += dot(m_cat[:, cols], z_buf[lax.rem(i, 2)])
+
+    blocks = n_ops // BLOCK
+    total[...] = jnp.zeros_like(total)
+    z_buf[...] = jnp.zeros_like(z_buf)
+    gather(jnp.int32(0))
+    scatter(jnp.int32(0))
+    gather(jnp.int32(1))
+
+    def steps(i, _):
+        apply(i - 2)
+        scatter(i - 1)
+        gather(i)
         return 0
 
-    lax.fori_loop(0, n_ops, gather_op, 0)
-    total[...] = dot(m_cat[...], z_cat[...])
+    lax.fori_loop(2, blocks, steps, 0)
+    apply(jnp.int32(blocks - 2))
+    scatter(jnp.int32(blocks - 1))
+    apply(jnp.int32(blocks - 1))
 
     left = iota((HALF, 128), 1) < 64
     for j in range(n_list):
@@ -290,8 +354,8 @@
     s = fin[me]
     for r in range(1, n_list):
         s = s + fin_buf[r - 1]
-    local_out[:HALF, :] = s[:, :64].astype(BF16)
-    local_out[HALF:, :] = pltpu.roll(s, 64, 1)[: NCOEF - HALF, :64].astype(BF16)
+    s = jnp.concatenate([s, pltpu.roll(s, 64, 1)], axis=0)
+    local_out[...] = s.T[:64, :NCOEF].astype(BF16)
 
 
 def per_device(
@@ -310,19 +374,26 @@
 ):
     slots = charge.shape[0]
     n_ops = m2l_ops.shape[0]
-    all_ops = n_ops + OCT
+    all_ops = SPREAD
     columns = LEAF + NEAR * CAP
     vmem = pl.BlockSpec(memory_space=pltpu.VMEM)
     dma = pltpu.SemaphoreType.DMA
-    return pl.pallas_call(
+    hbm = pl.BlockSpec(memory_space=pl.ANY)
+    local_t, tree_t = pl.pallas_call(
         functools.partial(kernel, n_leaf, n_list),
         out_shape=(
-            jax.ShapeDtypeStruct((NCOEF, LEAF // n_list), BF16),
-            jax.ShapeDtypeStruct((NCOEF, LEAF // 8 + LEAF // 64), BF16),
+            jax.ShapeDtypeStruct((LEAF // n_list, NCOEF), BF16),
+            jax.ShapeDtypeStruct((LEAF // 8 + LEAF // 64, NCOEF), BF16),
         ),
-        in_specs=[vmem] * 9 + [pl.BlockSpec(memory_space=pltpu.SMEM)],
+        in_specs=[hbm, hbm, vmem, vmem, hbm, hbm, vmem, hbm, hbm, pl.BlockSpec(memory_space=pltpu.SMEM)],
         out_specs=(vmem, vmem),
         scratch_shapes=[
+            pltpu.VMEM(charge.shape, F32),
+            pltpu.VMEM(position.shape, F32),
+            pltpu.VMEM(shift_ops.shape, BF16),
+            pltpu.VMEM(m2l_ops.shape, BF16),
+            pltpu.VMEM(list_src.shape[1:], jnp.int32),
+            pltpu.VMEM(list_src.shape[1:], jnp.int32),
             pltpu.VMEM((ORDER + 1, slots, LEAF), F32),
             pltpu.VMEM((ORDER + 1, slots, LEAF), F32),
             pltpu.VMEM((ORDER + 1, slots, LEAF), F32),
@@ -337,7 +408,8 @@
             pltpu.VMEM((ROWS, n_ops * WIDE), BF16),
             pltpu.VMEM((ROWS, OCT * WIDE), BF16),
             pltpu.VMEM((OCT * WIDE, 128), BF16),
-            pltpu.VMEM((n_ops * WIDE, LEAF), BF16),
+            pltpu.VMEM((2, BLOCK, ROWS, BATCH), BF16),
+            pltpu.VMEM((2, BLOCK * WIDE, LEAF), BF16),
             pltpu.VMEM((ROWS, LEAF), F32),
             pltpu.VMEM((n_list, HALF, 128), F32),
             pltpu.VMEM((n_list - 1, HALF, 128), F32),
@@ -349,6 +421,7 @@
             dma((NEAR,)),
             dma((n_list - 1,)),
             dma((n_list - 1,)),
+            dma((5 + IN_PARTS,)),
         ],
         compiler_params=pltpu.CompilerParams(
             collective_id=0, has_side_effects=True, vmem_limit_bytes=56 << 20
@@ -357,7 +430,7 @@
         charge,
         position,
         charge_count.reshape(1, -1),
-        octant.reshape(1, -1),
+        octant,
         shift_ops,
         m2l_ops,
         let_send[0],
@@ -365,6 +438,7 @@
         list_dst[0],
         batch_count,
     )
+    return local_t.T, tree_t.T
 
 
 def solution(mesh):

time: 76.7 us -> 51.9 us (0.68)
  Pallas kernels: 71.5 us -> 48.3 us
  local copies, waits for them, and re-layouts: 4.23 us -> 2.71 us
    pallas_call x1, Pallas kernels: 71.5 us -> 48.3 us  [per_device(): pl.pallas_call(functools.partial(kernel, n_leaf, n_list), out_shape=(jax....]
    pallas_call x2 -> x0, local copies, waits for them, and re-layouts: 2.98 us -> none  [per_device(): pl.pallas_call(functools.partial(kernel, n_leaf, n_list), out_shape=(jax....]
    unnamed x0 -> x2, local copies, waits for them, and re-layouts: none -> 2.71 us
    reshape x1 -> x0, local copies, waits for them, and re-layouts: 1.25 us -> none  [per_device(): octant.reshape(1, -1)]
where the time goes in v1:
time: 51.9 us; the launch traced here: 51.6 us
  Pallas kernels  48.3 us (93%)
  local copies, waits for them, and re-layouts  2.71 us (5%)
  between operations  0.64 us (1%)
    pallas_call x1, Pallas kernels, per_device(): pl.pallas_call(functools.partial(kernel, n_leaf, n_list), out_shape=(jax....  48.3 us
    unnamed x2, local copies, waits for them, and re-layouts  2.71 us

profile of v1, /device:TPU:1, one launch (start us, length us, event | category | flops | bytes accessed | tf_op | source)
XLA Modules:
  0.0 51.6 jit_solution(10220456605972009323)
XLA Ops:
  0.6 48.3 %shard_map.113 = (bf16[64,169]{1,0:T(8,128)(2,1)}, bf16[36,169]{1,0:T(8,128)(2,1)}) custom-call(f32[64,256]{1,0:T(8,128)} %charge_hbm.1, f32[3,64,256]{2,1,0:T(8,128)} %position_hbm.1, s32[1,256]{1,0:T(1,128)} %bitcast.11, s32[288]{0:T(512)} %octant.1, bf16[8,28672]{1,0:T(8,128)(2,1)} %shift_hbm.1, bf16[40,28672]{1,0:T(8,128)(2,1)} %m2l_hbm.1, ...), custom_call_target="tpu_custom_call" | custom-call | tf_op jit(solution)/shard_map/pallas_call | solution.py:382
  48.9 1.4 %copy.14 = bf16[169,64]{0,1:T(8,128)(2,1)} copy(bf16[169,64]{0,1:T(8,128)(2,1)} %bitcast.8) | data formatting | bytes 43264
  50.3 1.3 %copy.15 = bf16[169,36]{0,1:T(8,128)(2,1)} copy(bf16[169,36]{0,1:T(8,128)(2,1)} %bitcast.9) | data formatting | bytes 24336

commit v2 on v1

--- a/solution.py
+++ b/solution.py
@@ -18,8 +18,10 @@
 OCT = 8
 WIDE = 256
 HALF = ROWS // 2
-BLOCK = 4
+BLOCK = 8
 IN_PARTS = 4
+TILES = 1 + NEAR * CAP // LEAF
+PAIR = 2
 SPREAD = 56
 
 MESH = pl.DeviceIdType.MESH
@@ -79,6 +81,7 @@
     m_cat,
     s_cat,
     pick,
+    x_own,
     x_buf,
     z_buf,
     total,
@@ -232,16 +235,16 @@
     for copy in ag:
         copy.wait()
     leaves = multi[...].reshape(n_list * CHUNK, LEAF)[:ROWS]
-    table[:, :LEAF] = leaves
+    table[0] = leaves
 
     halo = []
     for k in (0, 7, 1, 6, 2, 5, 3, 4):
         pickers = onehot(iota((LEAF, CAP), 0) == let_send[k : k + 1, :])
         outgoing[k] = dot(leaves, pickers).astype(BF16)
-        to = LEAF + (NEAR - 1 - k) * CAP
+        to = NEAR - 1 - k
         copy = pltpu.make_async_remote_copy(
             src_ref=outgoing.at[k],
-            dst_ref=table.at[:, to : to + CAP],
+            dst_ref=table.at[1 + to // 2, :, to % 2 * CAP : to % 2 * CAP + CAP],
             send_sem=halo_send.at[k],
             recv_sem=halo_recv.at[k],
             device_id=(near_ids[k], me),
@@ -279,10 +282,8 @@
         pick[o * WIDE : o * WIDE + ROWS, :] = dot_nt(parents[:, :n_par], chosen).astype(BF16)
     grand = dot(s_cat[...], pick[...])
     tree = jnp.where(iota((ROWS, 128), 1) < n_par, parents.astype(F32), grand)
-    tree_out[...] = tree.T[: n_par + n_par // 8, :NCOEF].astype(BF16)
-
-    for copy in halo:
-        copy.wait()
+    tree_out[...] = tree
+
 
     for copy in lists_in:
         copy.wait()
@@ -291,15 +292,32 @@
         ids = iota((n, row.shape[1]), 0).astype(jnp.int16)
         return jnp.where(ids == (row - base).astype(jnp.int16), jnp.array(1, BF16), jnp.array(0, BF16))
 
+    def sources(g):
+        rows = []
+        for v in range(PAIR):
+            src = list_src[pl.ds(g + v, 1), :]
+            rows.append(jnp.where(iota((1, BATCH), 1) < batch_count[0, g + v], src, TILES * LEAF))
+        return jnp.concatenate(rows, axis=1)
+
+    def gather_own(p, _):
+        x_own[p] = dot(leaves, hot16(sources(p * PAIR), 0, LEAF)).astype(BF16)
+        return 0
+
+    lax.fori_loop(0, n_ops // PAIR, gather_own, 0, unroll=4)
+    for copy in halo:
+        copy.wait()
+
     def gather(i):
-        for u in range(BLOCK):
-            g = i * BLOCK + u
-            src = list_src[pl.ds(g, 1), :]
-            src = jnp.where(iota((1, BATCH), 1) < batch_count[0, g], src, -1)
-            x = jnp.zeros((ROWS, BATCH), F32)
-            for h in range(table.shape[1] // 256):
-                x = x + dot(table[:, h * 256 : h * 256 + 256], hot16(src, h * 256, 256))
-            x_buf[lax.rem(i, 2), u] = x.astype(BF16)
+        for u in range(0, BLOCK, PAIR):
+            src = sources(i * BLOCK + u)
+            tile = src // LEAF
+            others = table[1:].reshape((TILES - 1) * ROWS, LEAF)
+            each = dot(others, hot16(src - tile * LEAF, 0, LEAF))
+            x = x_own[i * (BLOCK // PAIR) + u // PAIR].astype(F32)
+            for h in range(1, TILES):
+                x = jnp.where(tile == h, each[(h - 1) * ROWS : h * ROWS], x)
+            for v in range(PAIR):
+                x_buf[lax.rem(i, 2), u + v] = x[:, v * BATCH : v * BATCH + BATCH].astype(BF16)
 
     def scatter(i):
         for u in range(BLOCK):
@@ -354,8 +372,14 @@
     s = fin[me]
     for r in range(1, n_list):
         s = s + fin_buf[r - 1]
+    local_out[...] = s
+
+
+def finish(local, tree, local_out, tree_out):
+    s = local[...]
     s = jnp.concatenate([s, pltpu.roll(s, 64, 1)], axis=0)
-    local_out[...] = s.T[:64, :NCOEF].astype(BF16)
+    local_out[...] = s.T[: local_out.shape[0], :NCOEF].astype(BF16)
+    tree_out[...] = tree[...].T[: tree_out.shape[0], :NCOEF].astype(BF16)
 
 
 def per_device(
@@ -375,15 +399,14 @@
     slots = charge.shape[0]
     n_ops = m2l_ops.shape[0]
     all_ops = SPREAD
-    columns = LEAF + NEAR * CAP
     vmem = pl.BlockSpec(memory_space=pltpu.VMEM)
     dma = pltpu.SemaphoreType.DMA
     hbm = pl.BlockSpec(memory_space=pl.ANY)
-    local_t, tree_t = pl.pallas_call(
+    local, tree = pl.pallas_call(
         functools.partial(kernel, n_leaf, n_list),
         out_shape=(
-            jax.ShapeDtypeStruct((LEAF // n_list, NCOEF), BF16),
-            jax.ShapeDtypeStruct((LEAF // 8 + LEAF // 64, NCOEF), BF16),
+            jax.ShapeDtypeStruct((HALF, 128), F32),
+            jax.ShapeDtypeStruct((ROWS, 128), F32),
         ),
         in_specs=[hbm, hbm, vmem, vmem, hbm, hbm, vmem, hbm, hbm, pl.BlockSpec(memory_space=pltpu.SMEM)],
         out_specs=(vmem, vmem),
@@ -402,12 +425,13 @@
             pltpu.VMEM((n_list - 1, CHUNK, LEAF), F32),
             pltpu.VMEM((n_list, CHUNK, LEAF), BF16),
             pltpu.VMEM((NEAR, ROWS, CAP), BF16),
-            pltpu.VMEM((ROWS, columns), BF16),
+            pltpu.VMEM((TILES, ROWS, LEAF), BF16),
             pltpu.VMEM((ROWS * all_ops, 128), F32),
             pltpu.VMEM((ROWS * all_ops, 128), F32),
             pltpu.VMEM((ROWS, n_ops * WIDE), BF16),
             pltpu.VMEM((ROWS, OCT * WIDE), BF16),
             pltpu.VMEM((OCT * WIDE, 128), BF16),
+            pltpu.VMEM((n_ops // PAIR, ROWS, PAIR * BATCH), BF16),
             pltpu.VMEM((2, BLOCK, ROWS, BATCH), BF16),
             pltpu.VMEM((2, BLOCK * WIDE, LEAF), BF16),
             pltpu.VMEM((ROWS, LEAF), F32),
@@ -438,6 +462,15 @@
         list_dst[0],
         batch_count,
     )
+    local_t, tree_t = pl.pallas_call(
+        finish,
+        out_shape=(
+            jax.ShapeDtypeStruct((LEAF // n_list, NCOEF), BF16),
+            jax.ShapeDtypeStruct((LEAF // 8 + LEAF // 64, NCOEF), BF16),
+        ),
+        in_specs=[vmem, vmem],
+        out_specs=(vmem, vmem),
+    )(local, tree)
     return local_t.T, tree_t.T
 
 

time: 51.9 us -> 47.4 us (0.913)
  local copies, waits for them, and re-layouts: 2.71 us -> 0 us
  Pallas kernels: 48.3 us -> 46.3 us
    pallas_call x1, Pallas kernels: 48.3 us -> 44.6 us  [per_device(): pl.pallas_call(functools.partial(kernel, n_leaf, n_list), out_shape=(jax....]
    unnamed x2 -> x0, local copies, waits for them, and re-layouts: 2.71 us -> none
    pallas_call x0 -> x1, Pallas kernels: none -> 1.69 us  [per_device(): pl.pallas_call(finish, out_shape=(jax.ShapeDtypeStruct((LEAF // n_list, N...]
where the time goes in v2:
time: 47.4 us; the launch traced here: 46.9 us
  Pallas kernels  46.3 us (98%)
  between operations  0.64 us (1%)
    pallas_call x1, Pallas kernels, per_device(): pl.pallas_call(functools.partial(kernel, n_leaf, n_list), out_shape=(jax....  44.6 us
    pallas_call x1, Pallas kernels, per_device(): pl.pallas_call(finish, out_shape=(jax.ShapeDtypeStruct((LEAF // n_list, N...  1.69 us

profile of v2, /device:TPU:1, one launch (start us, length us, event | category | flops | bytes accessed | tf_op | source)
XLA Modules:
  0.0 46.9 jit_solution(629478730456842024)
XLA Ops:
  0.6 44.6 %shard_map.113 = (f32[88,128]{1,0:T(8,128)}, f32[176,128]{1,0:T(8,128)}) custom-call(f32[64,256]{1,0:T(8,128)} %charge_hbm.1, f32[3,64,256]{2,1,0:T(8,128)} %position_hbm.1, s32[1,256]{1,0:T(1,128)} %bitcast.9, s32[288]{0:T(512)} %octant.1, bf16[8,28672]{1,0:T(8,128)(2,1)} %shift_hbm.1, bf16[40,28672]{1,0:T(8,128)(2,1)} %m2l_hbm.1, s32[8,128]{1,0:T(8,128)} %bitcast.8, ...), custom_call_target="tpu_custom_call" | custom-call | tf_op jit(solution)/shard_map/pallas_call | solution.py:405
  45.2 1.7 %shard_map.114 = (bf16[64,169]{1,0:T(8,128)(2,1)}, bf16[36,169]{1,0:T(8,128)(2,1)}) custom-call(f32[88,128]{1,0:T(8,128)} %get-tuple-element.6.local, f32[176,128]{1,0:T(8,128)} %get-tuple-element.7.tree), custom_call_target="tpu_custom_call" | custom-call | tf_op jit(solution)/shard_map/pallas_call | solution.py:465

commit v3 on v2

--- a/solution.py
+++ b/solution.py
@@ -20,8 +20,11 @@
 HALF = ROWS // 2
 BLOCK = 8
 IN_PARTS = 4
+ROWS_FIRST = 91
+OPS_FIRST = 20
+TREE = 48
 TILES = 1 + NEAR * CAP // LEAF
-PAIR = 2
+PAIR = 4
 SPREAD = 56
 
 MESH = pl.DeviceIdType.MESH
@@ -51,18 +54,23 @@
     n_list,
     charge_hbm,
     position_hbm,
+    count_hbm,
+    octant_hbm,
+    shift_hbm,
+    m2l_hbm,
+    let_hbm,
+    src_hbm,
+    dst_hbm,
+    batch_hbm,
+    local_out,
+    tree_hbm,
+    charge,
+    position,
     count,
     octant,
-    shift_hbm,
-    m2l_hbm,
     let_send,
-    src_hbm,
-    dst_hbm,
     batch_count,
-    local_out,
     tree_out,
-    charge,
-    position,
     shift_ops,
     m2l_ops,
     list_src,
@@ -109,6 +117,7 @@
     charges_in = [
         pltpu.make_async_copy(charge_hbm, charge, in_sem.at[0]),
         pltpu.make_async_copy(position_hbm, position, in_sem.at[1]),
+        pltpu.make_async_copy(count_hbm, count, in_sem.at[5 + IN_PARTS]),
     ]
     step = m2l_ops.shape[1] // IN_PARTS
     ops_in = [
@@ -122,9 +131,14 @@
     lists_in = [
         pltpu.make_async_copy(src_hbm, list_src, in_sem.at[3]),
         pltpu.make_async_copy(dst_hbm, list_dst, in_sem.at[4]),
+        pltpu.make_async_copy(batch_hbm, batch_count, in_sem.at[6 + IN_PARTS]),
+    ]
+    cells_in = [
+        pltpu.make_async_copy(let_hbm, let_send, in_sem.at[7 + IN_PARTS]),
+        pltpu.make_async_copy(octant_hbm, octant, in_sem.at[8 + IN_PARTS]),
     ]
     ops_in.append(pltpu.make_async_copy(shift_hbm, shift_ops, in_sem.at[2]))
-    for copy in charges_in + ops_in + lists_in:
+    for copy in charges_in + ops_in + lists_in + cells_in:
         copy.start()
 
     barrier = pltpu.get_barrier_semaphore()
@@ -185,31 +199,25 @@
     flat0[tail, :] = jnp.zeros(((ROWS - NCOEF) * all_ops, 128), F32)
     flat1[tail, :] = jnp.zeros(((ROWS - NCOEF) * all_ops, 128), F32)
 
-    def align_row(k, _):
-        start = k * NCOEF
-        first = start // 128
-        turn = start - first * 128
-        back = lax.rem(128 - turn, 128)
-        for ref, at in ((m2l_ops, 0), (shift_ops, n_ops)):
-            count_ops = ref.shape[0]
-            lanes = iota((count_ops, 128), 1)
-            pieces = [
-                pltpu.roll(
-                    ref[:, pl.ds(pl.multiple_of((first + i) * 128, 128), 128)].astype(F32), back, 1
-                )
-                for i in range(3)
-            ]
-            keep = lanes < 128 - turn
-            rows = pl.ds(pl.multiple_of(k * all_ops + at, 8), count_ops)
-            flat0[rows, :] = jnp.where(keep, pieces[0], pieces[1])
-            flat1[rows, :] = jnp.where(
-                lanes < NCOEF - 128, jnp.where(keep, pieces[1], pieces[2]), 0.0
-            )
-        return 0
+    def align_rows(ks):
+        for k in ks:
+            first, turn = divmod(k * NCOEF, 128)
+            for ref, at in ((m2l_ops, 0), (shift_ops, n_ops)):
+                count_ops = ref.shape[0]
+                lanes = iota((count_ops, 128), 1)
+                pieces = []
+                for i in range(2 if turn + NCOEF <= 256 else 3):
+                    piece = ref[:, (first + i) * 128 : (first + i + 1) * 128].astype(F32)
+                    pieces.append(pltpu.roll(piece, 128 - turn, 1) if turn else piece)
+                keep = lanes < 128 - turn
+                rest = pieces[1] if len(pieces) == 2 else jnp.where(keep, pieces[1], pieces[2])
+                rows = slice(k * all_ops + at, k * all_ops + at + count_ops)
+                flat0[rows, :] = jnp.where(keep, pieces[0], pieces[1])
+                flat1[rows, :] = jnp.where(lanes < NCOEF - 128, rest, 0.0)
 
     for copy in ops_in:
         copy.wait()
-    lax.fori_loop(0, 91, align_row, 0, unroll=13)
+    align_rows(range(ROWS_FIRST))
 
     for copy in rs:
         copy.wait()
@@ -230,8 +238,18 @@
         copy.start()
         ag.append(copy)
 
-    lax.fori_loop(91, NCOEF, align_row, 0, unroll=13)
-
+    align_rows(range(ROWS_FIRST, NCOEF))
+
+    def take_op(g, _):
+        cols = pl.multiple_of(g * WIDE, WIDE)
+        m_cat[:, pl.ds(cols, 128)] = flat0[pl.ds(g, ROWS, stride=all_ops), :].astype(BF16)
+        m_cat[:, pl.ds(cols + 128, 128)] = flat1[pl.ds(g, ROWS, stride=all_ops), :].astype(BF16)
+        return 0
+
+    lax.fori_loop(0, OPS_FIRST, take_op, 0, unroll=4)
+
+    for copy in cells_in:
+        copy.wait()
     for copy in ag:
         copy.wait()
     leaves = multi[...].reshape(n_list * CHUNK, LEAF)[:ROWS]
@@ -253,13 +271,7 @@
         copy.start()
         halo.append(copy)
 
-    def take_op(g, _):
-        cols = pl.multiple_of(g * WIDE, WIDE)
-        m_cat[:, pl.ds(cols, 128)] = flat0[pl.ds(g, ROWS, stride=all_ops), :].astype(BF16)
-        m_cat[:, pl.ds(cols + 128, 128)] = flat1[pl.ds(g, ROWS, stride=all_ops), :].astype(BF16)
-        return 0
-
-    lax.fori_loop(0, n_ops, take_op, 0, unroll=4)
+    lax.fori_loop(OPS_FIRST, n_ops, take_op, 0, unroll=4)
     for o in range(OCT):
         rows = pl.ds(n_ops + o, ROWS, stride=all_ops)
         s_cat[:, o * WIDE : o * WIDE + 128] = flat0[rows, :].astype(BF16)
@@ -282,7 +294,9 @@
         pick[o * WIDE : o * WIDE + ROWS, :] = dot_nt(parents[:, :n_par], chosen).astype(BF16)
     grand = dot(s_cat[...], pick[...])
     tree = jnp.where(iota((ROWS, 128), 1) < n_par, parents.astype(F32), grand)
-    tree_out[...] = tree
+    tree_out[...] = tree.T[:TREE, :NCOEF].astype(BF16)
+    tree_done = pltpu.make_async_copy(tree_out, tree_hbm, in_sem.at[9 + IN_PARTS])
+    tree_done.start()
 
 
     for copy in lists_in:
@@ -372,14 +386,14 @@
     s = fin[me]
     for r in range(1, n_list):
         s = s + fin_buf[r - 1]
-    local_out[...] = s
-
-
-def finish(local, tree, local_out, tree_out):
-    s = local[...]
     s = jnp.concatenate([s, pltpu.roll(s, 64, 1)], axis=0)
     local_out[...] = s.T[: local_out.shape[0], :NCOEF].astype(BF16)
-    tree_out[...] = tree[...].T[: tree_out.shape[0], :NCOEF].astype(BF16)
+    tree_done.wait()
+
+
+def finish(local, tree, local_out, tree_out):
+    local_out[...] = local[...]
+    tree_out[...] = tree[: tree_out.shape[0], :]
 
 
 def per_device(
@@ -405,14 +419,19 @@
     local, tree = pl.pallas_call(
         functools.partial(kernel, n_leaf, n_list),
         out_shape=(
-            jax.ShapeDtypeStruct((HALF, 128), F32),
-            jax.ShapeDtypeStruct((ROWS, 128), F32),
+            jax.ShapeDtypeStruct((LEAF // n_list, NCOEF), BF16),
+            jax.ShapeDtypeStruct((TREE, NCOEF), BF16),
         ),
-        in_specs=[hbm, hbm, vmem, vmem, hbm, hbm, vmem, hbm, hbm, pl.BlockSpec(memory_space=pltpu.SMEM)],
-        out_specs=(vmem, vmem),
+        in_specs=[hbm] * 10,
+        out_specs=(vmem, hbm),
         scratch_shapes=[
             pltpu.VMEM(charge.shape, F32),
             pltpu.VMEM(position.shape, F32),
+            pltpu.VMEM((1, LEAF), jnp.int32),
+            pltpu.VMEM(octant.shape, jnp.int32),
+            pltpu.VMEM(let_send.shape[1:], jnp.int32),
+            pltpu.SMEM(batch_count.shape, jnp.int32),
+            pltpu.VMEM((TREE, NCOEF), BF16),
             pltpu.VMEM(shift_ops.shape, BF16),
             pltpu.VMEM(m2l_ops.shape, BF16),
             pltpu.VMEM(list_src.shape[1:], jnp.int32),
@@ -445,7 +464,7 @@
             dma((NEAR,)),
             dma((n_list - 1,)),
             dma((n_list - 1,)),
-            dma((5 + IN_PARTS,)),
+            dma((10 + IN_PARTS,)),
         ],
         compiler_params=pltpu.CompilerParams(
             collective_id=0, has_side_effects=True, vmem_limit_bytes=56 << 20

time: 47.4 us -> 45.5 us (0.960)
  Pallas kernels: 46.3 us -> 44.7 us
    pallas_call x1, Pallas kernels: 44.6 us -> 43.3 us  [per_device(): pl.pallas_call(functools.partial(kernel, n_leaf, n_list), out_shape=(jax....]
where the time goes in v3:
time: 45.5 us; the launch traced here: 45.3 us
  Pallas kernels  44.7 us (98%)
  between operations  0.64 us (1%)
    pallas_call x1, Pallas kernels, per_device(): pl.pallas_call(functools.partial(kernel, n_leaf, n_list), out_shape=(jax....  43.3 us
    pallas_call x1, Pallas kernels, per_device(): pl.pallas_call(finish, out_shape=(jax.ShapeDtypeStruct((LEAF // n_list, N...  1.38 us

profile of v3, /device:TPU:1, one launch (start us, length us, event | category | flops | bytes accessed | tf_op | source)
XLA Modules:
  0.0 45.3 jit_solution(12696418594214385980)
XLA Ops:
  0.6 43.3 %shard_map.113 = (bf16[64,169]{1,0:T(8,128)(2,1)}, bf16[48,169]{1,0:T(8,128)(2,1)}) custom-call(f32[64,256]{1,0:T(8,128)} %charge_hbm.1, f32[3,64,256]{2,1,0:T(8,128)} %position_hbm.1, s32[1,256]{1,0:T(1,128)} %bitcast.9, s32[288]{0:T(512)} %octant_hbm.1, bf16[8,28672]{1,0:T(8,128)(2,1)} %shift_hbm.1, bf16[40,28672]{1,0:T(8,128)(2,1)} %m2l_hbm.1, ...), custom_call_target="tpu_custom_call" | custom-call | tf_op jit(solution)/shard_map/pallas_call | solution.py:419
  43.9 1.4 %shard_map.114 = (bf16[64,169]{1,0:T(8,128)(2,1)}, bf16[36,169]{1,0:T(8,128)(2,1)}) custom-call(bf16[64,169]{1,0:T(8,128)(2,1)} %get-tuple-element.6.local, bf16[48,169]{1,0:T(8,128)(2,1)} %get-tuple-element.7.tree), custom_call_target="tpu_custom_call" | custom-call | tf_op jit(solution)/shard_map/pallas_call | solution.py:484

commit v4 on v3

--- a/solution.py
+++ b/solution.py
@@ -24,7 +24,7 @@
 OPS_FIRST = 20
 TREE = 48
 TILES = 1 + NEAR * CAP // LEAF
-PAIR = 4
+PAIR = 2
 SPREAD = 56
 
 MESH = pl.DeviceIdType.MESH
@@ -39,6 +39,11 @@
 
 def onehot(mask):
     return jnp.where(mask, 1.0, 0.0).astype(BF16)
+
+
+def hot16(row, base, n):
+    ids = iota((n, row.shape[1]), 0).astype(jnp.int16)
+    return jnp.where(ids == (row - base).astype(jnp.int16), jnp.array(1, BF16), jnp.array(0, BF16))
 
 
 def dot(a, b):
@@ -82,6 +87,7 @@
     part,
     rs_buf,
     multi,
+    pickers,
     outgoing,
     table,
     flat0,
@@ -113,6 +119,7 @@
     offsets = [k - NEAR // 2 if k < NEAR // 2 else k - NEAR // 2 + 1 for k in range(NEAR)]
     near_ids = [lax.rem(me_leaf + off + n_leaf, n_leaf) for off in offsets]
     peers = [lax.rem(me + r, n_list) for r in range(1, n_list)]
+    far_first = sorted(range(1, n_list), key=lambda r: -min(r, n_list - r))
 
     charges_in = [
         pltpu.make_async_copy(charge_hbm, charge, in_sem.at[0]),
@@ -183,7 +190,7 @@
     pl.semaphore_wait(barrier, NEAR + n_list - 1)
 
     rs = []
-    for r in range(1, n_list):
+    for r in far_first:
         copy = pltpu.make_async_remote_copy(
             src_ref=part.at[peers[r - 1]],
             dst_ref=rs_buf.at[r - 1],
@@ -226,7 +233,7 @@
         mine = mine + rs_buf[r - 1]
     multi[me] = mine.astype(BF16)
     ag = []
-    for r in range(1, n_list):
+    for r in far_first:
         copy = pltpu.make_async_remote_copy(
             src_ref=multi.at[me],
             dst_ref=multi.at[me],
@@ -250,15 +257,17 @@
 
     for copy in cells_in:
         copy.wait()
+    for k in range(NEAR):
+        pickers[:, k * CAP : k * CAP + CAP] = hot16(let_send[k : k + 1, :], 0, LEAF)
     for copy in ag:
         copy.wait()
     leaves = multi[...].reshape(n_list * CHUNK, LEAF)[:ROWS]
     table[0] = leaves
 
+    picked = dot(leaves, pickers[...]).astype(BF16)
     halo = []
     for k in (0, 7, 1, 6, 2, 5, 3, 4):
-        pickers = onehot(iota((LEAF, CAP), 0) == let_send[k : k + 1, :])
-        outgoing[k] = dot(leaves, pickers).astype(BF16)
+        outgoing[k] = picked[:, k * CAP : k * CAP + CAP]
         to = NEAR - 1 - k
         copy = pltpu.make_async_remote_copy(
             src_ref=outgoing.at[k],
@@ -272,6 +281,84 @@
         halo.append(copy)
 
     lax.fori_loop(OPS_FIRST, n_ops, take_op, 0, unroll=4)
+    for copy in lists_in:
+        copy.wait()
+
+    def sources(g):
+        rows = []
+        for v in range(PAIR):
+            src = list_src[pl.ds(g + v, 1), :]
+            rows.append(jnp.where(iota((1, BATCH), 1) < batch_count[0, g + v], src, TILES * LEAF))
+        return jnp.concatenate(rows, axis=1)
+
+    def gather_own(p, _):
+        x_own[p] = dot(leaves, hot16(sources(p * PAIR), 0, LEAF)).astype(BF16)
+        return 0
+
+    lax.fori_loop(0, n_ops // PAIR, gather_own, 0, unroll=4)
+    for copy in halo:
+        copy.wait()
+
+    def gather(i):
+        for u in range(0, BLOCK, PAIR):
+            src = sources(i * BLOCK + u)
+            tile = src // LEAF
+            others = table[1:].reshape((TILES - 1) * ROWS, LEAF)
+            each = dot(others, hot16(src - tile * LEAF, 0, LEAF))
+            x = x_own[i * (BLOCK // PAIR) + u // PAIR].astype(F32)
+            for h in range(1, TILES):
+                x = jnp.where(tile == h, each[(h - 1) * ROWS : h * ROWS], x)
+            for v in range(PAIR):
+                x_buf[lax.rem(i, 2), u + v] = x[:, v * BATCH : v * BATCH + BATCH].astype(BF16)
+
+    def scatter(i):
+        for u in range(BLOCK):
+            dst = list_dst[pl.ds(i * BLOCK + u, 1), :]
+            z = dot_nt(x_buf[lax.rem(i, 2), u], hot16(dst, 0, LEAF))
+            z_buf[lax.rem(i, 2), u * WIDE : u * WIDE + ROWS, :] = z.astype(BF16)
+
+    def apply(i):
+        cols = pl.ds(pl.multiple_of(i * (BLOCK * WIDE), BLOCK * WIDE), BLOCK * WIDE)
+        total[...] += dot(m_cat[:, cols], z_buf[lax.rem(i, 2)])
+
+    blocks = n_ops // BLOCK
+    total[...] = jnp.zeros_like(total)
+    z_buf[...] = jnp.zeros_like(z_buf)
+    gather(jnp.int32(0))
+    scatter(jnp.int32(0))
+    gather(jnp.int32(1))
+
+    def steps(i, _):
+        apply(i - 2)
+        scatter(i - 1)
+        gather(i)
+        return 0
+
+    lax.fori_loop(2, blocks, steps, 0)
+    apply(jnp.int32(blocks - 2))
+    scatter(jnp.int32(blocks - 1))
+    apply(jnp.int32(blocks - 1))
+
+    left = iota((HALF, 128), 1) < 64
+    for j in range(n_list):
+        cols = slice(j // 2 * 128, j // 2 * 128 + 128)
+        top, low = total[:HALF, cols], total[HALF:, cols]
+        if j % 2 == 0:
+            fin[j] = jnp.where(left, top, pltpu.roll(low, 64, 1))
+        else:
+            fin[j] = jnp.where(left, pltpu.roll(top, 64, 1), low)
+    last = []
+    for r in far_first:
+        copy = pltpu.make_async_remote_copy(
+            src_ref=fin.at[peers[r - 1]],
+            dst_ref=fin_buf.at[r - 1],
+            send_sem=fin_send.at[r - 1],
+            recv_sem=fin_recv.at[r - 1],
+            device_id=(me_leaf, peers[r - 1]),
+            device_id_type=MESH,
+        )
+        copy.start()
+        last.append(copy)
     for o in range(OCT):
         rows = pl.ds(n_ops + o, ROWS, stride=all_ops)
         s_cat[:, o * WIDE : o * WIDE + 128] = flat0[rows, :].astype(BF16)
@@ -299,88 +386,6 @@
     tree_done.start()
 
 
-    for copy in lists_in:
-        copy.wait()
-
-    def hot16(row, base, n):
-        ids = iota((n, row.shape[1]), 0).astype(jnp.int16)
-        return jnp.where(ids == (row - base).astype(jnp.int16), jnp.array(1, BF16), jnp.array(0, BF16))
-
-    def sources(g):
-        rows = []
-        for v in range(PAIR):
-            src = list_src[pl.ds(g + v, 1), :]
-            rows.append(jnp.where(iota((1, BATCH), 1) < batch_count[0, g + v], src, TILES * LEAF))
-        return jnp.concatenate(rows, axis=1)
-
-    def gather_own(p, _):
-        x_own[p] = dot(leaves, hot16(sources(p * PAIR), 0, LEAF)).astype(BF16)
-        return 0
-
-    lax.fori_loop(0, n_ops // PAIR, gather_own, 0, unroll=4)
-    for copy in halo:
-        copy.wait()
-
-    def gather(i):
-        for u in range(0, BLOCK, PAIR):
-            src = sources(i * BLOCK + u)
-            tile = src // LEAF
-            others = table[1:].reshape((TILES - 1) * ROWS, LEAF)
-            each = dot(others, hot16(src - tile * LEAF, 0, LEAF))
-            x = x_own[i * (BLOCK // PAIR) + u // PAIR].astype(F32)
-            for h in range(1, TILES):
-                x = jnp.where(tile == h, each[(h - 1) * ROWS : h * ROWS], x)
-            for v in range(PAIR):
-                x_buf[lax.rem(i, 2), u + v] = x[:, v * BATCH : v * BATCH + BATCH].astype(BF16)
-
-    def scatter(i):
-        for u in range(BLOCK):
-            dst = list_dst[pl.ds(i * BLOCK + u, 1), :]
-            z = dot_nt(x_buf[lax.rem(i, 2), u], hot16(dst, 0, LEAF))
-            z_buf[lax.rem(i, 2), u * WIDE : u * WIDE + ROWS, :] = z.astype(BF16)
-
-    def apply(i):
-        cols = pl.ds(pl.multiple_of(i * (BLOCK * WIDE), BLOCK * WIDE), BLOCK * WIDE)
-        total[...] += dot(m_cat[:, cols], z_buf[lax.rem(i, 2)])
-
-    blocks = n_ops // BLOCK
-    total[...] = jnp.zeros_like(total)
-    z_buf[...] = jnp.zeros_like(z_buf)
-    gather(jnp.int32(0))
-    scatter(jnp.int32(0))
-    gather(jnp.int32(1))
-
-    def steps(i, _):
-        apply(i - 2)
-        scatter(i - 1)
-        gather(i)
-        return 0
-
-    lax.fori_loop(2, blocks, steps, 0)
-    apply(jnp.int32(blocks - 2))
-    scatter(jnp.int32(blocks - 1))
-    apply(jnp.int32(blocks - 1))
-
-    left = iota((HALF, 128), 1) < 64
-    for j in range(n_list):
-        cols = slice(j // 2 * 128, j // 2 * 128 + 128)
-        top, low = total[:HALF, cols], total[HALF:, cols]
-        if j % 2 == 0:
-            fin[j] = jnp.where(left, top, pltpu.roll(low, 64, 1))
-        else:
-            fin[j] = jnp.where(left, pltpu.roll(top, 64, 1), low)
-    last = []
-    for r in range(1, n_list):
-        copy = pltpu.make_async_remote_copy(
-            src_ref=fin.at[peers[r - 1]],
-            dst_ref=fin_buf.at[r - 1],
-            send_sem=fin_send.at[r - 1],
-            recv_sem=fin_recv.at[r - 1],
-            device_id=(me_leaf, peers[r - 1]),
-            device_id_type=MESH,
-        )
-        copy.start()
-        last.append(copy)
     for copy in last:
         copy.wait()
     s = fin[me]
@@ -443,6 +448,7 @@
             pltpu.VMEM((n_list, CHUNK, LEAF), F32),
             pltpu.VMEM((n_list - 1, CHUNK, LEAF), F32),
             pltpu.VMEM((n_list, CHUNK, LEAF), BF16),
+            pltpu.VMEM((LEAF, NEAR * CAP), BF16),
             pltpu.VMEM((NEAR, ROWS, CAP), BF16),
             pltpu.VMEM((TILES, ROWS, LEAF), BF16),
             pltpu.VMEM((ROWS * all_ops, 128), F32),

time: 45.5 us -> 44.6 us (0.980)
  Pallas kernels: 44.7 us -> 43.8 us
    pallas_call x1, Pallas kernels: 43.3 us -> 42.4 us  [per_device(): pl.pallas_call(functools.partial(kernel, n_leaf, n_list), out_shape=(jax....]
where the time goes in v4:
time: 44.6 us; the launch traced here: 44.4 us
  Pallas kernels  43.8 us (98%)
  between operations  0.64 us (1%)
    pallas_call x1, Pallas kernels, per_device(): pl.pallas_call(functools.partial(kernel, n_leaf, n_list), out_shape=(jax....  42.4 us
    pallas_call x1, Pallas kernels, per_device(): pl.pallas_call(finish, out_shape=(jax.ShapeDtypeStruct((LEAF // n_list, N...  1.38 us

profile of v4, /device:TPU:1, one launch (start us, length us, event | category | flops | bytes accessed | tf_op | source)
XLA Modules:
  0.0 44.4 jit_solution(17608323349127594003)
XLA Ops:
  0.6 42.4 %shard_map.113 = (bf16[64,169]{1,0:T(8,128)(2,1)}, bf16[48,169]{1,0:T(8,128)(2,1)}) custom-call(f32[64,256]{1,0:T(8,128)} %charge_hbm.1, f32[3,64,256]{2,1,0:T(8,128)} %position_hbm.1, s32[1,256]{1,0:T(1,128)} %bitcast.9, s32[288]{0:T(512)} %octant_hbm.1, bf16[8,28672]{1,0:T(8,128)(2,1)} %shift_hbm.1, bf16[40,28672]{1,0:T(8,128)(2,1)} %m2l_hbm.1, ...), custom_call_target="tpu_custom_call" | custom-call | tf_op jit(solution)/shard_map/pallas_call | solution.py:424
  43.0 1.4 %shard_map.114 = (bf16[64,169]{1,0:T(8,128)(2,1)}, bf16[36,169]{1,0:T(8,128)(2,1)}) custom-call(bf16[64,169]{1,0:T(8,128)(2,1)} %get-tuple-element.6.local, bf16[48,169]{1,0:T(8,128)(2,1)} %get-tuple-element.7.tree), custom_call_target="tpu_custom_call" | custom-call | tf_op jit(solution)/shard_map/pallas_call | solution.py:490

commit v5 on v4

--- a/solution.py
+++ b/solution.py
@@ -18,7 +18,7 @@
 OCT = 8
 WIDE = 256
 HALF = ROWS // 2
-BLOCK = 8
+BLOCK = 10
 IN_PARTS = 4
 ROWS_FIRST = 91
 OPS_FIRST = 20

time: 44.6 us -> 44.5 us (level)
  no operation moved by 1% of the time
where the time goes in v5:
time: 44.5 us; the launch traced here: 44.3 us
  Pallas kernels  43.6 us (98%)
  between operations  0.64 us (1%)
    pallas_call x1, Pallas kernels, per_device(): pl.pallas_call(functools.partial(kernel, n_leaf, n_list), out_shape=(jax....  42.2 us
    pallas_call x1, Pallas kernels, per_device(): pl.pallas_call(finish, out_shape=(jax.ShapeDtypeStruct((LEAF // n_list, N...  1.38 us

profile of v5, /device:TPU:1, one launch (start us, length us, event | category | flops | bytes accessed | tf_op | source)
XLA Modules:
  0.0 44.3 jit_solution(11674124134269668636)
XLA Ops:
  0.6 42.2 %shard_map.113 = (bf16[64,169]{1,0:T(8,128)(2,1)}, bf16[48,169]{1,0:T(8,128)(2,1)}) custom-call(f32[64,256]{1,0:T(8,128)} %charge_hbm.1, f32[3,64,256]{2,1,0:T(8,128)} %position_hbm.1, s32[1,256]{1,0:T(1,128)} %bitcast.9, s32[288]{0:T(512)} %octant_hbm.1, bf16[8,28672]{1,0:T(8,128)(2,1)} %shift_hbm.1, bf16[40,28672]{1,0:T(8,128)(2,1)} %m2l_hbm.1, ...), custom_call_target="tpu_custom_call" | custom-call | tf_op jit(solution)/shard_map/pallas_call | solution.py:424
  42.9 1.4 %shard_map.114 = (bf16[64,169]{1,0:T(8,128)(2,1)}, bf16[36,169]{1,0:T(8,128)(2,1)}) custom-call(bf16[64,169]{1,0:T(8,128)(2,1)} %get-tuple-element.6.local, bf16[48,169]{1,0:T(8,128)(2,1)} %get-tuple-element.7.tree), custom_call_target="tpu_custom_call" | custom-call | tf_op jit(solution)/shard_map/pallas_call | solution.py:490
